TPU v7x, 32 devices: a whole 2x2x4 slice. The times are simulated.
32 devices in a mesh: ctx: 8 (over y, x, core), head: 4 (over z).
Axes of the slice: x: 2, y: 2, z: 4, core: 2. Of those that a mesh axis runs over, the one named last changes fastest.
Arguments:
- query_rows: bfloat16 [4096, 2048], P('ctx', 'head'), may hold values from -245 to 245
- key_rows: bfloat16 [4096, 2048], P('ctx', 'head'), may hold values from -20.5 to 20.5
- value_rows: bfloat16 [4096, 2048], P('ctx', 'head'), may hold values from -6 to 6
- segment_ids: int32 [4096], replicated, may hold values from 0 to 63, never falling along the last dimension, each value on 1 to 256 neighbouring positions
- out_weight: bfloat16 [2048, 2048], P('head'), may hold values from -0.375 to 0.375
- emg_signal: bfloat16 [64, 4096], P(None, 'ctx'), may hold values from -6 to 6
- stencil_taps: bfloat16 [5, 64, 4096], P(None, None, 'ctx'), may hold values from -4 to 4
- emg_weight: bfloat16 [64, 2048], replicated, may hold values from -0.75 to 0.75
- out_grad: bfloat16 [4096, 2048], P('ctx', 'head'), may hold values from -6 to 6
Outputs:
- layer_out: bfloat16 [4096, 2048], P('ctx', 'head')
- grad_queries: bfloat16 [4096, 2048], P('ctx', 'head')
- grad_keys: bfloat16 [4096, 2048], P('ctx', 'head')
- grad_values: bfloat16 [4096, 2048], P('ctx', 'head')
- grad_emg: bfloat16 [64, 4096], P(None, 'ctx')
Inputs may be any that keep to these rules, and one draw needn't show every extreme that they name: `segment_ids`: segment ids never fall along the sequence, and every id from 0 to the largest occurs.
All inputs are finite; a program needn't handle non-finite values.
Results may differ from a plain program's by a relative error of at most 0.03.
Values may be sent and summed in bfloat16 or wider, within the bound.
A program may use at most 128 MiB of HBM per device.

v0:
```python
import jax
import jax.numpy as jnp
from jax import lax
from jax.sharding import PartitionSpec as P

DH = 128
REACH = 2
TAPS = 5


MASKED = -1e30


def with_halo(value, sides, width):
    for axis, dim in sides:
        count, length = (lax.axis_size(axis), value.shape[dim])
        up = [(i, (i + 1) % count) for i in range(count - 1)]
        down = [(j, i) for i, j in up]
        last = lax.slice_in_dim(value, length - width, length, axis=dim)
        leading = lax.slice_in_dim(value, 0, width, axis=dim)
        before = lax.ppermute(last, axis, up)
        after = lax.ppermute(leading, axis, down)
        value = jnp.concatenate([before, value, after], axis=dim)
    return value


def shifted(value, axis, steps):
    count = lax.axis_size(axis)
    pairs = [(source, (source + steps) % count) for source in range(count)]
    return lax.ppermute(value, axis, pairs)


def block_source(anchor, turn_index, cycle_size):
    return (anchor - turn_index + cycle_size) % cycle_size


def gradient_block(
    query_heads, grad_heads, log_total, row_delta, query_segs, key_heads, value_heads, key_segs
):
    score_scale = DH ** (-0.5)
    scores = (
        jnp.einsum("qhd,khd->hqk", query_heads, key_heads, preferred_element_type=jnp.float32)
        * score_scale
    )
    allowed = (key_segs[None, :] <= query_segs[:, None])[None]
    scores = jnp.where(allowed, scores, MASKED)
    probs = jnp.where(allowed, jnp.exp(scores - log_total[:, :, None]), 0.0)
    weight_grad = jnp.einsum(
        "qhd,khd->hqk", grad_heads, value_heads, preferred_element_type=jnp.float32
    )
    score_grad = (probs * (weight_grad - row_delta[:, :, None])).astype(jnp.bfloat16)
    value_part = jnp.einsum(
        "hqk,qhd->khd", probs.astype(jnp.bfloat16), grad_heads, preferred_element_type=jnp.float32
    )
    key_part = jnp.einsum(
        "hqk,qhd->khd", score_grad, query_heads, preferred_element_type=jnp.float32
    )
    query_part = jnp.einsum(
        "hqk,khd->qhd", score_grad, key_heads, preferred_element_type=jnp.float32
    )
    return (query_part, key_part, value_part)


def body(
    query_rows,
    key_rows,
    value_rows,
    segment_ids,
    out_weight,
    emg_signal,
    stencil_taps,
    emg_weight,
    out_grad,
):
    tok_rows = query_rows.shape[0]
    head_count = query_rows.shape[1] // DH
    channel_count = emg_weight.shape[0]
    score_scale = DH ** (-0.5)
    cycle_size = lax.axis_size("ctx")
    anchor = lax.axis_index("ctx")
    query_segs = lax.dynamic_slice_in_dim(segment_ids, anchor * tok_rows, tok_rows)
    query_heads = query_rows.reshape(tok_rows, head_count, DH)
    key_heads = key_rows.reshape(tok_rows, head_count, DH)
    value_heads = value_rows.reshape(tok_rows, head_count, DH)
    row_top = jnp.full((head_count, tok_rows), MASKED, jnp.float32)
    accumulated = jnp.zeros((tok_rows, head_count, DH), jnp.float32)
    block_keys = lax.all_gather(key_rows, "ctx", axis=0, tiled=True)
    block_values = lax.all_gather(value_rows, "ctx", axis=0, tiled=True)
    block_len = block_keys.shape[0]
    key_segs = segment_ids
    keys_here = block_keys.reshape(block_len, head_count, DH)
    values_here = block_values.reshape(block_len, head_count, DH)
    scores = (
        jnp.einsum("qhd,khd->hqk", query_heads, keys_here, preferred_element_type=jnp.float32)
        * score_scale
    )
    allowed = (key_segs[None, :] <= query_segs[:, None])[None]
    scores = jnp.where(allowed, scores, MASKED)
    new_top = jnp.maximum(row_top, jnp.max(scores, axis=2))
    weights = jnp.where(allowed, jnp.exp(scores - new_top[:, :, None]), 0.0)
    factor = jnp.exp(row_top - new_top)
    new_total = jnp.sum(weights, axis=2)
    mixed = jnp.einsum(
        "hqk,khd->qhd",
        weights.astype(jnp.bfloat16),
        values_here,
        preferred_element_type=jnp.float32,
    )
    new_accum = accumulated * factor.T[:, :, None] + mixed
    log_total = new_top + jnp.log(new_total)
    attended = (new_accum / new_total.T[:, :, None]).astype(jnp.bfloat16)
    attn_rows = attended.reshape(tok_rows, head_count * DH)
    extended = with_halo(emg_signal, (("ctx", 1),), REACH)
    filtered = jnp.zeros((channel_count, tok_rows), jnp.float32)
    for tap_index in range(TAPS):
        filtered = filtered + stencil_taps[tap_index].astype(jnp.float32) * extended[
            :, tap_index : tap_index + tok_rows
        ].astype(jnp.float32)
    filtered = filtered.astype(jnp.bfloat16)
    partial_out = jnp.dot(attn_rows, out_weight, preferred_element_type=jnp.float32)
    reduced = lax.psum_scatter(
        partial_out.astype(jnp.bfloat16), "head", scatter_dimension=1, tiled=True
    ).astype(jnp.float32)
    col_width = reduced.shape[1]
    emg_cols = lax.dynamic_slice_in_dim(
        emg_weight, lax.axis_index("head") * col_width, col_width, 1
    )
    stencil_out = lax.dot_general(
        filtered, emg_cols, (((0,), (0,)), ((), ())), preferred_element_type=jnp.float32
    )
    layer_out = (reduced + stencil_out).astype(jnp.bfloat16)
    grad_cols = lax.all_gather(out_grad, "head", axis=1, tiled=True)
    attn_acc = lax.dot_general(
        grad_cols, out_weight, (((1,), (1,)), ((), ())), preferred_element_type=jnp.float32
    )
    filter_acc = lax.dot_general(
        emg_weight, grad_cols, (((1,), (1,)), ((), ())), preferred_element_type=jnp.float32
    )
    attn_acc, filter_acc = (attn_acc, filter_acc)
    attn_grad = attn_acc.astype(jnp.bfloat16)
    filter_grad = filter_acc.astype(jnp.bfloat16)
    grad_heads = attn_grad.reshape(tok_rows, head_count, DH)
    row_delta = jnp.sum(grad_heads.astype(jnp.float32) * attended.astype(jnp.float32), axis=2).T
    stacked = jnp.concatenate([filter_grad[None], stencil_taps], axis=0)
    widened = with_halo(stacked, (("ctx", 2),), REACH)
    emg_acc = jnp.zeros((channel_count, tok_rows), jnp.float32)
    for tap_index in range(TAPS):
        lower_edge = 2 * REACH - tap_index
        emg_acc = emg_acc + widened[1 + tap_index, :, lower_edge : lower_edge + tok_rows].astype(
            jnp.float32
        ) * widened[0, :, lower_edge : lower_edge + tok_rows].astype(jnp.float32)
    grad_emg = emg_acc.astype(jnp.bfloat16)
    zero_heads = jnp.zeros((tok_rows, head_count, DH), jnp.float32)

    def key_turn(turn_index, state_in):
        moving_keys, moving_values, key_grad, value_grad, query_grad = state_in
        source = block_source(anchor, turn_index, cycle_size)
        key_segs = lax.dynamic_slice_in_dim(segment_ids, source * tok_rows, tok_rows)
        query_part, key_part, value_part = gradient_block(
            query_heads,
            grad_heads,
            log_total,
            row_delta,
            query_segs,
            moving_keys,
            moving_values,
            key_segs,
        )
        moving_keys, moving_values = shifted((moving_keys, moving_values), "ctx", 1)
        key_grad, value_grad = (
            shifted((key_grad + key_part).astype(jnp.bfloat16), "ctx", 1).astype(jnp.float32),
            shifted((value_grad + value_part).astype(jnp.bfloat16), "ctx", 1).astype(jnp.float32),
        )
        return (moving_keys, moving_values, key_grad, value_grad, query_grad + query_part)

    final_state = lax.fori_loop(
        0, cycle_size, key_turn, (key_heads, value_heads, zero_heads, zero_heads, zero_heads)
    )
    key_grad, value_grad, query_grad = (final_state[2], final_state[3], final_state[4])
    grad_queries = (
        (query_grad * score_scale).astype(jnp.bfloat16).reshape(tok_rows, head_count * DH)
    )
    grad_keys = (key_grad * score_scale).astype(jnp.bfloat16).reshape(tok_rows, head_count * DH)
    grad_values = value_grad.astype(jnp.bfloat16).reshape(tok_rows, head_count * DH)
    return (layer_out, grad_queries, grad_keys, grad_values, grad_emg)


def solution(mesh):
    in_specs = (
        P("ctx", "head"),
        P("ctx", "head"),
        P("ctx", "head"),
        P(),
        P("head", None),
        P(None, "ctx"),
        P(None, None, "ctx"),
        P(),
        P("ctx", "head"),
    )
    out_specs = (
        P("ctx", "head"),
        P("ctx", "head"),
        P("ctx", "head"),
        P("ctx", "head"),
        P(None, "ctx"),
    )
    return jax.shard_map(body, mesh=mesh, in_specs=in_specs, out_specs=out_specs, check_vma=False)
```

profile of v0, /device:TPU:8, one launch (start us, length us, event | category | flops | bytes accessed | tf_op | source)
XLA Modules:
  0.0 488.4 jit_solution(1443986999030061492)
XLA Ops:
  28.0 27.1 %all-gather.8.cloned.1.call-done = bf16[512,2048]{1,0:T(8,128)(2,1)} async-done(((bf16[512,512]{1,0:T(8,128)(2,1)}), bf16[512,2048]{1,0:T(8,128)(2,1)}) %all-gather.8.cloned.1.call-update) | async-done | bytes 2097168 | tf_op jit(solution)/shard_map/all_gather | solution.py:132
  69.4 26.2 %all-gather.4.cloned.1.call-done = bf16[4096,512]{0,1:T(8,128)(2,1)} async-done(((bf16[512,512]{0,1:T(8,128)(2,1)}), bf16[4096,512]{0,1:T(8,128)(2,1)}) %all-gather.4.cloned.1.call-update) | async-done | bytes 4194320 | tf_op jit(solution)/shard_map/all_gather | solution.py:87
  95.6 17.6 %fusion.19 = (f32[4,512]{1,0:T(4,128)S(1)}, f32[4,512,4096]{2,1,0:T(8,128)}) fusion(pred[512,4096]{1,0:T(8,128)(4,1)} %broadcast_compare_fusion.1, bf16[512,4,128]{0,2,1:T(8,128)(2,1)S(1)} %bitcast.130, bf16[4096,4,128]{0,2,1:T(8,128)(2,1)} %bitcast.132), kind=kOutput, calls=%fused_computation.19 | convolution fusion | flops 2172647424 | bytes 40378368 | tf_op jit(solution)/shard_map/qhd,khd->hqk/dot_general | solution.py:94
  113.2 15.9 %fusion.20 = f32[4,512]{1,0:T(4,128)S(1)} fusion(f32[4,512,4096]{2,1,0:T(8,128)} %get-tuple-element.420, f32[4,512]{1,0:T(4,128)S(1)} %broadcast_maximum_fusion, pred[512,4096]{1,0:T(8,128)(4,1)S(1)} %copy-done.4), kind=kLoop, calls=%fused_computation.20 | loop fusion | flops 41940992 | bytes 35667968 | tf_op jit(solution)/shard_map/reduce_sum | solution.py:102
  129.1 5.1 %all-gather.6.cloned.1.call-done = bf16[4096,512]{1,0:T(8,128)(2,1)} async-done(((bf16[512,512]{1,0:T(8,128)(2,1)}), bf16[4096,512]{1,0:T(8,128)(2,1)}) %all-gather.6.cloned.1.call-update) | async-done | bytes 4194320 | tf_op jit(solution)/shard_map/all_gather | solution.py:88
  134.2 6.4 %copy.27 = bf16[4096,512]{0,1:T(8,128)(2,1)} copy(bf16[4096,512]{1,0:T(8,128)(2,1)} %all-gather.6.cloned.1.call-done) | data formatting | bytes 8388608 | tf_op jit(solution)/shard_map/all_gather | solution.py:88
  140.6 16.5 %multiply_reduce_fusion = (f32[512,4]{0,1:T(4,128)S(1)}, bf16[512,4,128]{0,2,1:T(8,128)(2,1)S(1)}) fusion(bf16[512,512]{0,1:T(8,128)(2,1)S(1)} %copy-done.8, f32[512,4]{0,1:T(4,128)S(1)} %bitcast.140, bf16[4096,4,128]{0,2,1:T(8,128)(2,1)} %bitcast.133, f32[4,512,4096]{2,1,0:T(8,128)} %get-tuple-element.420, f32[4,512]{1,0:T(4,128)S(1)} %broadcast_maximum_fusion, ...), kind=kOutput, calls=%fused_computation.34 | convolution fusion | flops 2191259648 | bytes 40927232 | tf_op jit(solution)/shard_map/hqk,khd->qhd/dot_general | solution.py:103
  159.8 313.9 %while.24 = (s32[]{:T(128)}, bf16[512,4,128]{2,0,1:T(8,128)(2,1)}, bf16[512,4,128]{2,0,1:T(8,128)(2,1)}, f32[512,4,128]{2,0,1:T(8,128)}, f32[512,4,128]{2,0,1:T(...) while((s32[]{:T(128)}, bf16[512,4,128]{2,0,1:T(8,128)(2,1)}, ...), condition=%wide.region_5.6_spmd.clone, body=%wide.region_4.5_spmd.clone.sunk | while | flops 1357643776 | bytes 69501568 | solution.py:176
  166.7 4.3 multiply_convert_fusion.4
  193.7 5.6 %collective-permute-done.1 = bf16[512,4,128]{2,0,1:T(8,128)(2,1)} collective-permute-done((bf16[512,4,128]{2,0,1:T(8,128)(2,1)}, bf16[512,4,128]{2,0,1:T(8,128)(2,1)}, u32[]{:S(2)}, u32[]{:S(2)}) %collective-permute-start.1) | collective-permute-done | bytes 524320 | tf_op jit(solution)/shard_map/while/body/eval_jaxpr/ppermute | solution.py:30
  205.9 4.3 multiply_convert_fusion.4
  232.9 5.6 %collective-permute-done.1 = bf16[512,4,128]{2,0,1:T(8,128)(2,1)} collective-permute-done((bf16[512,4,128]{2,0,1:T(8,128)(2,1)}, bf16[512,4,128]{2,0,1:T(8,128)(2,1)}, u32[]{:S(2)}, u32[]{:S(2)}) %collective-permute-start.1) | collective-permute-done | bytes 524320 | tf_op jit(solution)/shard_map/while/body/eval_jaxpr/ppermute | solution.py:30
  245.1 4.3 multiply_convert_fusion.4
  272.1 5.6 %collective-permute-done.1 = bf16[512,4,128]{2,0,1:T(8,128)(2,1)} collective-permute-done((bf16[512,4,128]{2,0,1:T(8,128)(2,1)}, bf16[512,4,128]{2,0,1:T(8,128)(2,1)}, u32[]{:S(2)}, u32[]{:S(2)}) %collective-permute-start.1) | collective-permute-done | bytes 524320 | tf_op jit(solution)/shard_map/while/body/eval_jaxpr/ppermute | solution.py:30
  284.3 4.3 multiply_convert_fusion.4
  311.3 5.6 %collective-permute-done.1 = bf16[512,4,128]{2,0,1:T(8,128)(2,1)} collective-permute-done((bf16[512,4,128]{2,0,1:T(8,128)(2,1)}, bf16[512,4,128]{2,0,1:T(8,128)(2,1)}, u32[]{:S(2)}, u32[]{:S(2)}) %collective-permute-start.1) | collective-permute-done | bytes 524320 | tf_op jit(solution)/shard_map/while/body/eval_jaxpr/ppermute | solution.py:30
  323.5 4.3 multiply_convert_fusion.4
  350.5 5.6 %collective-permute-done.1 = bf16[512,4,128]{2,0,1:T(8,128)(2,1)} collective-permute-done((bf16[512,4,128]{2,0,1:T(8,128)(2,1)}, bf16[512,4,128]{2,0,1:T(8,128)(2,1)}, u32[]{:S(2)}, u32[]{:S(2)}) %collective-permute-start.1) | collective-permute-done | bytes 524320 | tf_op jit(solution)/shard_map/while/body/eval_jaxpr/ppermute | solution.py:30
  362.7 4.3 multiply_convert_fusion.4
  389.7 5.6 %collective-permute-done.1 = bf16[512,4,128]{2,0,1:T(8,128)(2,1)} collective-permute-done((bf16[512,4,128]{2,0,1:T(8,128)(2,1)}, bf16[512,4,128]{2,0,1:T(8,128)(2,1)}, u32[]{:S(2)}, u32[]{:S(2)}) %collective-permute-start.1) | collective-permute-done | bytes 524320 | tf_op jit(solution)/shard_map/while/body/eval_jaxpr/ppermute | solution.py:30
  401.9 4.3 multiply_convert_fusion.4
  428.9 5.6 %collective-permute-done.1 = bf16[512,4,128]{2,0,1:T(8,128)(2,1)} collective-permute-done((bf16[512,4,128]{2,0,1:T(8,128)(2,1)}, bf16[512,4,128]{2,0,1:T(8,128)(2,1)}, u32[]{:S(2)}, u32[]{:S(2)}) %collective-permute-start.1) | collective-permute-done | bytes 524320 | tf_op jit(solution)/shard_map/while/body/eval_jaxpr/ppermute | solution.py:30
  441.1 4.3 multiply_convert_fusion.4
  468.1 5.6 %collective-permute-done.1 = bf16[512,4,128]{2,0,1:T(8,128)(2,1)} collective-permute-done((bf16[512,4,128]{2,0,1:T(8,128)(2,1)}, bf16[512,4,128]{2,0,1:T(8,128)(2,1)}, u32[]{:S(2)}, u32[]{:S(2)}) %collective-permute-start.1) | collective-permute-done | bytes 524320 | tf_op jit(solution)/shard_map/while/body/eval_jaxpr/ppermute | solution.py:30
  (260 shorter events, 279.6 us)
Async XLA Ops:
  7.2 47.9 %all-gather.8.cloned.1.call-start = ((), (), s32[]{:S(2)}) async-start(), calls=%async_computation.4 | async-start | bytes 2621440 | tf_op jit(solution)/shard_map/all_gather | solution.py:132
  7.9 87.6 %all-gather.4.cloned.1.call-start = ((), (), s32[]{:S(2)}) async-start(), calls=%async_computation.1 | async-start | bytes 4718592 | tf_op jit(solution)/shard_map/all_gather | solution.py:87
  10.0 124.2 %all-gather.6.cloned.1.call-start = ((), (), s32[]{:S(2)}) async-start(), calls=%async_computation.2 | async-start | bytes 4718592 | tf_op jit(solution)/shard_map/all_gather | solution.py:88
  10.8 468.7 %reduce-scatter.2.cloned.1.call-start = ((), (), s32[]{:S(2)}) async-start(), calls=%async_computation.3 | async-start | bytes 2621440 | tf_op jit(solution)/shard_map/reduce_scatter | solution.py:121
  12.2 467.2 %collective-permute-start.4 = (bf16[64,2]{1,0:T(8,128)(2,1)}, bf16[64,2]{1,0:T(8,128)(2,1)}, u32[]{:S(2)}, u32[]{:S(2)}) collective-permute-start(bf16[64,2]{1,0:T(8,128)(2,1)} %get-tuple-element.416), channel_id=1, source_target_pairs={{0,4},{4,8},{8,12},{12,16},{16,20},{20,24},{24,28},{1,5},{5,9},{9,... | collective-permute-start | bytes 776 | tf_op jit(solution)/shard_map/ppermute | solution.py:21
  176.9 16.8 %collective-permute-start = (bf16[512,4,128]{2,0,1:T(8,128)(2,1)S(1)}, bf16[512,4,128]{2,0,1:T(8,128)(2,1)}, u32[]{:S(2)}, u32[]{:S(2)}) collective-permute-start(bf16[512,4,128]{2,0,1:T(8,128)(2,1)S(1)} %copy.57), channel_id=1, source_target_pairs={{0,4},{4,8},{8,12},{12,16},{16,20},{20,24},{24,28},{28,0},{1,5},{5... | collective-permute-start | bytes 1572872 | tf_op jit(solution)/shard_map/while/body/eval_jaxpr/ppermute | solution.py:30
  177.6 21.7 %collective-permute-start.1 = (bf16[512,4,128]{2,0,1:T(8,128)(2,1)}, bf16[512,4,128]{2,0,1:T(8,128)(2,1)}, u32[]{:S(2)}, u32[]{:S(2)}) collective-permute-start(bf16[512,4,128]{2,0,1:T(8,128)(2,1)} %copy.58), channel_id=1, source_target_pairs={{0,4},{4,8},{8,12},{12,16},{16,20},{20,24},{24,28},{28,0},{1,5},{5... | collective-permute-start | bytes 1572872 | tf_op jit(solution)/shard_map/while/body/eval_jaxpr/ppermute | solution.py:30
  215.2 12.1 %collective-permute-start.3 = (bf16[512,4,128]{2,0,1:T(8,128)(2,1)}, bf16[512,4,128]{2,0,1:T(8,128)(2,1)}, u32[]{:S(2)}, u32[]{:S(2)}) collective-permute-start(bf16[512,4,128]{2,0,1:T(8,128)(2,1)} %fusion.112), channel_id=1, source_target_pairs={{0,4},{4,8},{8,12},{12,16},{16,20},{20,24},{24,28},{28,0},{1,5},{5... | collective-permute-start | bytes 1572872 | tf_op jit(solution)/shard_map/while/body/eval_jaxpr/ppermute | solution.py:30
  215.2 17.7 %collective-permute-start = (bf16[512,4,128]{2,0,1:T(8,128)(2,1)S(1)}, bf16[512,4,128]{2,0,1:T(8,128)(2,1)}, u32[]{:S(2)}, u32[]{:S(2)}) collective-permute-start(bf16[512,4,128]{2,0,1:T(8,128)(2,1)S(1)} %copy.57), channel_id=1, source_target_pairs={{0,4},{4,8},{8,12},{12,16},{16,20},{20,24},{24,28},{28,0},{1,5},{5... | collective-permute-start | bytes 1572872 | tf_op jit(solution)/shard_map/while/body/eval_jaxpr/ppermute | solution.py:30
  215.9 22.6 %collective-permute-start.1 = (bf16[512,4,128]{2,0,1:T(8,128)(2,1)}, bf16[512,4,128]{2,0,1:T(8,128)(2,1)}, u32[]{:S(2)}, u32[]{:S(2)}) collective-permute-start(bf16[512,4,128]{2,0,1:T(8,128)(2,1)} %copy.58), channel_id=1, source_target_pairs={{0,4},{4,8},{8,12},{12,16},{16,20},{20,24},{24,28},{28,0},{1,5},{5... | collective-permute-start | bytes 1572872 | tf_op jit(solution)/shard_map/while/body/eval_jaxpr/ppermute | solution.py:30
  254.4 12.1 %collective-permute-start.3 = (bf16[512,4,128]{2,0,1:T(8,128)(2,1)}, bf16[512,4,128]{2,0,1:T(8,128)(2,1)}, u32[]{:S(2)}, u32[]{:S(2)}) collective-permute-start(bf16[512,4,128]{2,0,1:T(8,128)(2,1)} %fusion.112), channel_id=1, source_target_pairs={{0,4},{4,8},{8,12},{12,16},{16,20},{20,24},{24,28},{28,0},{1,5},{5... | collective-permute-start | bytes 1572872 | tf_op jit(solution)/shard_map/while/body/eval_jaxpr/ppermute | solution.py:30
  254.4 17.7 %collective-permute-start = (bf16[512,4,128]{2,0,1:T(8,128)(2,1)S(1)}, bf16[512,4,128]{2,0,1:T(8,128)(2,1)}, u32[]{:S(2)}, u32[]{:S(2)}) collective-permute-start(bf16[512,4,128]{2,0,1:T(8,128)(2,1)S(1)} %copy.57), channel_id=1, source_target_pairs={{0,4},{4,8},{8,12},{12,16},{16,20},{20,24},{24,28},{28,0},{1,5},{5... | collective-permute-start | bytes 1572872 | tf_op jit(solution)/shard_map/while/body/eval_jaxpr/ppermute | solution.py:30
  254.4 23.3 %collective-permute-start.1 = (bf16[512,4,128]{2,0,1:T(8,128)(2,1)}, bf16[512,4,128]{2,0,1:T(8,128)(2,1)}, u32[]{:S(2)}, u32[]{:S(2)}) collective-permute-start(bf16[512,4,128]{2,0,1:T(8,128)(2,1)} %copy.58), channel_id=1, source_target_pairs={{0,4},{4,8},{8,12},{12,16},{16,20},{20,24},{24,28},{28,0},{1,5},{5... | collective-permute-start | bytes 1572872 | tf_op jit(solution)/shard_map/while/body/eval_jaxpr/ppermute | solution.py:30
  293.6 12.1 %collective-permute-start.3 = (bf16[512,4,128]{2,0,1:T(8,128)(2,1)}, bf16[512,4,128]{2,0,1:T(8,128)(2,1)}, u32[]{:S(2)}, u32[]{:S(2)}) collective-permute-start(bf16[512,4,128]{2,0,1:T(8,128)(2,1)} %fusion.112), channel_id=1, source_target_pairs={{0,4},{4,8},{8,12},{12,16},{16,20},{20,24},{24,28},{28,0},{1,5},{5... | collective-permute-start | bytes 1572872 | tf_op jit(solution)/shard_map/while/body/eval_jaxpr/ppermute | solution.py:30
  293.6 17.7 %collective-permute-start = (bf16[512,4,128]{2,0,1:T(8,128)(2,1)S(1)}, bf16[512,4,128]{2,0,1:T(8,128)(2,1)}, u32[]{:S(2)}, u32[]{:S(2)}) collective-permute-start(bf16[512,4,128]{2,0,1:T(8,128)(2,1)S(1)} %copy.57), channel_id=1, source_target_pairs={{0,4},{4,8},{8,12},{12,16},{16,20},{20,24},{24,28},{28,0},{1,5},{5... | collective-permute-start | bytes 1572872 | tf_op jit(solution)/shard_map/while/body/eval_jaxpr/ppermute | solution.py:30
  293.6 23.3 %collective-permute-start.1 = (bf16[512,4,128]{2,0,1:T(8,128)(2,1)}, bf16[512,4,128]{2,0,1:T(8,128)(2,1)}, u32[]{:S(2)}, u32[]{:S(2)}) collective-permute-start(bf16[512,4,128]{2,0,1:T(8,128)(2,1)} %copy.58), channel_id=1, source_target_pairs={{0,4},{4,8},{8,12},{12,16},{16,20},{20,24},{24,28},{28,0},{1,5},{5... | collective-permute-start | bytes 1572872 | tf_op jit(solution)/shard_map/while/body/eval_jaxpr/ppermute | solution.py:30
  332.8 17.7 %collective-permute-start = (bf16[512,4,128]{2,0,1:T(8,128)(2,1)S(1)}, bf16[512,4,128]{2,0,1:T(8,128)(2,1)}, u32[]{:S(2)}, u32[]{:S(2)}) collective-permute-start(bf16[512,4,128]{2,0,1:T(8,128)(2,1)S(1)} %copy.57), channel_id=1, source_target_pairs={{0,4},{4,8},{8,12},{12,16},{16,20},{20,24},{24,28},{28,0},{1,5},{5... | collective-permute-start | bytes 1572872 | tf_op jit(solution)/shard_map/while/body/eval_jaxpr/ppermute | solution.py:30
  332.8 23.3 %collective-permute-start.1 = (bf16[512,4,128]{2,0,1:T(8,128)(2,1)}, bf16[512,4,128]{2,0,1:T(8,128)(2,1)}, u32[]{:S(2)}, u32[]{:S(2)}) collective-permute-start(bf16[512,4,128]{2,0,1:T(8,128)(2,1)} %copy.58), channel_id=1, source_target_pairs={{0,4},{4,8},{8,12},{12,16},{16,20},{20,24},{24,28},{28,0},{1,5},{5... | collective-permute-start | bytes 1572872 | tf_op jit(solution)/shard_map/while/body/eval_jaxpr/ppermute | solution.py:30
  372.0 17.7 %collective-permute-start = (bf16[512,4,128]{2,0,1:T(8,128)(2,1)S(1)}, bf16[512,4,128]{2,0,1:T(8,128)(2,1)}, u32[]{:S(2)}, u32[]{:S(2)}) collective-permute-start(bf16[512,4,128]{2,0,1:T(8,128)(2,1)S(1)} %copy.57), channel_id=1, source_target_pairs={{0,4},{4,8},{8,12},{12,16},{16,20},{20,24},{24,28},{28,0},{1,5},{5... | collective-permute-start | bytes 1572872 | tf_op jit(solution)/shard_map/while/body/eval_jaxpr/ppermute | solution.py:30
  372.0 23.3 %collective-permute-start.1 = (bf16[512,4,128]{2,0,1:T(8,128)(2,1)}, bf16[512,4,128]{2,0,1:T(8,128)(2,1)}, u32[]{:S(2)}, u32[]{:S(2)}) collective-permute-start(bf16[512,4,128]{2,0,1:T(8,128)(2,1)} %copy.58), channel_id=1, source_target_pairs={{0,4},{4,8},{8,12},{12,16},{16,20},{20,24},{24,28},{28,0},{1,5},{5... | collective-permute-start | bytes 1572872 | tf_op jit(solution)/shard_map/while/body/eval_jaxpr/ppermute | solution.py:30
  411.2 17.7 %collective-permute-start = (bf16[512,4,128]{2,0,1:T(8,128)(2,1)S(1)}, bf16[512,4,128]{2,0,1:T(8,128)(2,1)}, u32[]{:S(2)}, u32[]{:S(2)}) collective-permute-start(bf16[512,4,128]{2,0,1:T(8,128)(2,1)S(1)} %copy.57), channel_id=1, source_target_pairs={{0,4},{4,8},{8,12},{12,16},{16,20},{20,24},{24,28},{28,0},{1,5},{5... | collective-permute-start | bytes 1572872 | tf_op jit(solution)/shard_map/while/body/eval_jaxpr/ppermute | solution.py:30
  411.2 23.3 %collective-permute-start.1 = (bf16[512,4,128]{2,0,1:T(8,128)(2,1)}, bf16[512,4,128]{2,0,1:T(8,128)(2,1)}, u32[]{:S(2)}, u32[]{:S(2)}) collective-permute-start(bf16[512,4,128]{2,0,1:T(8,128)(2,1)} %copy.58), channel_id=1, source_target_pairs={{0,4},{4,8},{8,12},{12,16},{16,20},{20,24},{24,28},{28,0},{1,5},{5... | collective-permute-start | bytes 1572872 | tf_op jit(solution)/shard_map/while/body/eval_jaxpr/ppermute | solution.py:30
  450.4 17.7 %collective-permute-start = (bf16[512,4,128]{2,0,1:T(8,128)(2,1)S(1)}, bf16[512,4,128]{2,0,1:T(8,128)(2,1)}, u32[]{:S(2)}, u32[]{:S(2)}) collective-permute-start(bf16[512,4,128]{2,0,1:T(8,128)(2,1)S(1)} %copy.57), channel_id=1, source_target_pairs={{0,4},{4,8},{8,12},{12,16},{16,20},{20,24},{24,28},{28,0},{1,5},{5... | collective-permute-start | bytes 1572872 | tf_op jit(solution)/shard_map/while/body/eval_jaxpr/ppermute | solution.py:30
  450.4 23.3 %collective-permute-start.1 = (bf16[512,4,128]{2,0,1:T(8,128)(2,1)}, bf16[512,4,128]{2,0,1:T(8,128)(2,1)}, u32[]{:S(2)}, u32[]{:S(2)}) collective-permute-start(bf16[512,4,128]{2,0,1:T(8,128)(2,1)} %copy.58), channel_id=1, source_target_pairs={{0,4},{4,8},{8,12},{12,16},{16,20},{20,24},{24,28},{28,0},{1,5},{5... | collective-permute-start | bytes 1572872 | tf_op jit(solution)/shard_map/while/body/eval_jaxpr/ppermute | solution.py:30
  (56 other events, 474.2 us)
Sparse Core Ops, SparseCore 0:
  9.6 45.4 all-gather.7
  57.5 37.9 all-gather.3
  97.5 36.7 all-gather.5
  159.9 41.6 reduce-scatter.1
where the time goes:
time: 493 us; the launch traced here: 488 us
  waiting for transfers between devices  172 us (35%)
  matrix products  157 us (32%)
  other arithmetic  60.7 us (12%)
  local copies, waits for them, and re-layouts  57.4 us (12%)
  starting transfers between devices  26.1 us (5%)
  between operations  13.9 us (3%)
    ppermute x32, waiting for transfers between devices, shifted(): return lax.ppermute(value, axis, pairs)  113 us
    dot_general x8, matrix products, gradient_block(): jnp.einsum('qhd,khd->hqk', grad_heads, value_heads, preferred_element_typ...  34.2 us
    while x80, local copies, waits for them, and re-layouts  28.9 us
    all_gather x1, waiting for transfers between devices, body(): grad_cols = lax.all_gather(out_grad, 'head', axis=1, tiled=True)  27.1 us
    all_gather x1, waiting for transfers between devices, body(): block_keys = lax.all_gather(key_rows, 'ctx', axis=0, tiled=True)  26.2 us
    dot_general x8, matrix products, gradient_block(): jnp.einsum('hqk,khd->qhd', score_grad, key_heads, preferred_element_type=...  22.4 us
    dot_general x8, matrix products, gradient_block(): jnp.einsum('qhd,khd->hqk', query_heads, key_heads, preferred_element_type...  21.3 us
    dot_general x8, matrix products, gradient_block(): jnp.einsum('hqk,qhd->khd', probs.astype(jnp.bfloat16), grad_heads, prefer...  20.9 us
  transfers between devices with their start and end apart: 40, of which 35 were waited for; matrix products, arithmetic and copies ran while one was open for 55% of the time, Pallas kernels for 0%

commit v1 on v0

v1 whole, which is shorter than its diff:
```python
import functools
import math

import jax
import jax.numpy as jnp
from jax import lax
from jax.experimental import pallas as pl
from jax.experimental.pallas import tpu as pltpu
from jax.sharding import PartitionSpec as P

DH = 128
REACH = 2
TAPS = 5
MAX_SEG = 256
EDGE = 128
MASKED = -1e30
LOG2E = math.log2(math.e)
MESH = pl.DeviceIdType.MESH
BF16 = jnp.bfloat16
F32 = jnp.float32


def dot(a, b, ca=1, cb=0):
    return lax.dot_general(a, b, (((ca,), (cb,)), ((), ())), preferred_element_type=F32)


def kernel(
    n, m, hc, g,
    q_ref, k_ref, v_ref, segq_ref, segk_ref, w_ref, emg_ref, taps_ref, ew_ref, do_ref,
    out_ref, dq_ref, dk_ref, dv_ref, demg_ref,
    qg, kg, vg, kt, vt, og, lse_s, ar, po, pr, dg, acc_s, ag, dog,
    dka, dva, dqs, dks, dvs, dkr, dvr, emg_pad, taps_pad, fg_pad,
    s_in, r_in, s_ar, r_ar, s_dg, r_dg, s_po, r_po, s_do, r_do,
    s_dq, r_dq, s_kv, r_kv, s_halo, r_halo,
):
    me = lax.axis_index("ctx")
    hd = lax.axis_index("head")
    tok = q_ref.shape[0]
    tile = tok // g
    colw = do_ref.shape[1]
    my_h, my_s = me // g, me % g
    scale = DH ** (-0.5)

    def cols(h):
        return pl.ds(pl.multiple_of(h * DH, DH), DH)

    def rows(s):
        return pl.ds(pl.multiple_of(s * tile, tile), tile)

    def wide(d):
        return pl.ds(pl.multiple_of(d * colw, colw), colw)

    def remote(src, dst, ssem, rsem, **target):
        return pltpu.make_async_remote_copy(
            src_ref=src, dst_ref=dst, send_sem=ssem, recv_sem=rsem,
            device_id=target, device_id_type=MESH,
        )

    barrier = pltpu.get_barrier_semaphore()

    @pl.loop(1, n)
    def _(d):
        pl.semaphore_signal(barrier, inc=1, device_id={"ctx": (me + d) % n}, device_id_type=MESH)

    @pl.loop(1, m)
    def _(d):
        pl.semaphore_signal(barrier, inc=1, device_id={"head": (hd + d) % m}, device_id_type=MESH)

    pl.semaphore_wait(barrier, n - 1 + m - 1)

    def in_copies(t, src):
        h, s = t // g, t % g
        return (
            remote(k_ref.at[:, cols(h)], kg.at[src], s_in.at[0, t], r_in.at[0, src], ctx=t),
            remote(q_ref.at[rows(s), cols(h)], qg.at[src], s_in.at[1, t], r_in.at[1, src], ctx=t),
            remote(v_ref.at[:, cols(h)], vg.at[src], s_in.at[2, t], r_in.at[2, src], ctx=t),
        )

    def dg_copy(t, src):
        return remote(do_ref, dg.at[src], s_dg.at[t], r_dg.at[src], head=t)

    def po_copy(t, src):
        return remote(po.at[t], pr.at[src], s_po.at[t], r_po.at[src], head=t)

    def do_copy(t, src):
        return remote(ag.at[rows(t % g), cols(t // g)], dog.at[src], s_do.at[t], r_do.at[src], ctx=t)

    def ar_copy(t, src):
        return remote(og.at[t], ar.at[rows(src % g), cols(src // g)], s_ar.at[t], r_ar.at[src], ctx=t)

    def dq_copy(t, src):
        return remote(dqs.at[t], dq_ref.at[rows(src % g), cols(src // g)], s_dq.at[t], r_dq.at[src], ctx=t)

    def kv_copies(t, src):
        return (
            remote(dks.at[t], dkr.at[src], s_kv.at[0, t], r_kv.at[0, src], ctx=t),
            remote(dvs.at[t], dvr.at[src], s_kv.at[1, t], r_kv.at[1, src], ctx=t),
        )

    right, left = (me + 1) % n, (me + n - 1) % n
    last = EDGE + tok

    def halo_copies(index, pad, lead):
        def at(lo):
            return pad.at[lead + (slice(None), pl.ds(lo, EDGE))]

        return (
            remote(at(last - EDGE), at(0), s_halo.at[index, 0], r_halo.at[index, 0], ctx=right),
            remote(at(EDGE), at(last), s_halo.at[index, 1], r_halo.at[index, 1], ctx=left),
        )

    @pl.loop(1, m)
    def _(d):
        dg_copy((hd + d) % m, hd).start()

    @pl.loop(1, n)
    def _(d):
        for copy in in_copies((me + d) % n, me):
            copy.start()

    kg[me] = k_ref[:, cols(my_h)]
    vg[me] = v_ref[:, cols(my_h)]
    qg[me] = q_ref[rows(my_s), cols(my_h)]
    dg[hd] = do_ref[...]
    emg_pad[:, EDGE:last] = emg_ref[...]
    taps_pad[:, :, EDGE:last] = taps_ref[...]
    halos = halo_copies(0, emg_pad, ()) + halo_copies(1, taps_pad, (slice(None),))
    for copy in halos:
        copy.start()
    dka[...] = jnp.zeros_like(dka)
    dva[...] = jnp.zeros_like(dva)

    def arrive(b):
        @pl.when(b != me)
        def _():
            for copy in in_copies(me, b):
                copy.wait_recv()

        kt[b] = kg[b].T
        vt[b] = vg[b].T

    half = min(MAX_SEG, tok)
    need_next = ((my_s + 1) * tile + MAX_SEG - 1 > tok).astype(jnp.int32)

    def scores_of(b, c, count, masked, q):
        st = dot(kg[c, pl.ds(0, count), :], q, 1, 1) * (scale * LOG2E)
        if masked:
            segq = segq_ref[b * g + my_s]
            segk = segk_ref[c, pl.ds(0, count), :]
            st = jnp.where(segk <= segq, st, MASKED)
        return st

    def extra_of(b):
        return jnp.where(b + 1 < n, need_next, 0)

    arrive(0)

    def forward_tile(b, unused):
        @pl.when(b + 1 < n)
        def _():
            arrive(b + 1)

        q = qg[b]

        def step(c, state, count=tok, masked=False):
            top, total, acc = state
            st = scores_of(b, c, count, masked, q)
            new_top = jnp.maximum(top, jnp.max(st, axis=0, keepdims=True))
            p = jnp.exp2(st - new_top)
            factor = jnp.exp2(top - new_top)
            total = total * factor + jnp.sum(p, axis=0, keepdims=True)
            acc = acc * factor + dot(vt[c, :, pl.ds(0, count)], p.astype(BF16))
            return new_top, total, acc

        state = (
            jnp.full((1, tile), MASKED, F32),
            jnp.zeros((1, tile), F32),
            jnp.zeros((DH, tile), F32),
        )
        state = lax.fori_loop(0, b, step, state)
        state = step(b, state, masked=True)
        state = lax.fori_loop(
            0, extra_of(b), lambda i, s: step(b + 1, s, count=half, masked=True), state
        )
        top, total, acc = state
        lse_s[b] = top + jnp.log2(total)
        result = (acc / total).T.astype(BF16)
        og[b] = result

        @pl.when(b == me)
        def _():
            ar[rows(my_s), cols(my_h)] = result

        @pl.when(b != me)
        def _():
            ar_copy(b, me).start()

        return unused

    lax.fori_loop(0, n, forward_tile, 0)

    @pl.loop(1, n)
    def _(d):
        ar_copy(me, (me + d) % n).wait_recv()

    @pl.loop(1, m + 1)
    def _(d):
        t = (hd + d) % m
        part = dot(ar[...], w_ref[:, wide(t)]).astype(BF16)

        @pl.when(t == hd)
        def _():
            pr[hd] = part

        @pl.when(t != hd)
        def _():
            po[t] = part
            po_copy(t, hd).start()

    acc_s[...] = jnp.zeros_like(acc_s)
    channels = ew_ref.shape[0]

    def grad_turn(d, filter_acc):
        src = (hd + d) % m

        @pl.when(d > 0)
        def _():
            dg_copy(hd, src).wait_recv()

        block = dg[src]
        acc_s[...] += dot(block, w_ref[:, wide(src)], 1, 1)
        return filter_acc + dot(ew_ref[:, wide(src)], block, 1, 1)

    filter_acc = lax.fori_loop(0, m, grad_turn, jnp.zeros((channels, tok), F32))
    ag[...] = acc_s[...].astype(BF16)

    @pl.loop(1, n)
    def _(d):
        do_copy((me + d) % n, me).start()

    dog[me] = ag[rows(my_s), cols(my_h)]
    fg_pad[:, EDGE:last] = filter_acc.astype(BF16)
    fg_halos = halo_copies(2, fg_pad, ())
    for copy in fg_halos:
        copy.start()

    def send_kv(c):
        key_part, value_part = dka[c].astype(BF16), dva[c].astype(BF16)

        @pl.when(c == me)
        def _():
            dkr[me] = key_part
            dvr[me] = value_part

        @pl.when(c != me)
        def _():
            dks[c] = key_part
            dvs[c] = value_part
            for copy in kv_copies(c, me):
                copy.start()

    def backward_tile(turn, unused):
        b = n - 1 - turn

        @pl.when(b != me)
        def _():
            do_copy(me, b).wait_recv()

        q, do, lse = qg[b], dog[b], lse_s[b]
        delta = jnp.sum((do.astype(F32) * og[b].astype(F32)).T, axis=0, keepdims=True)

        def step(c, dqt, count=tok, masked=False):
            keys = pl.ds(0, count)
            st = scores_of(b, c, count, masked, q)
            p = jnp.exp2(st - lse)
            dpt = dot(vg[c, keys, :], do, 1, 1)
            ds = (p * (dpt - delta)).astype(BF16)
            dva[c, keys, :] += dot(p.astype(BF16), do)
            dka[c, keys, :] += dot(ds, q)
            return dqt + dot(kt[c, :, keys], ds)

        dqt = lax.fori_loop(
            0, extra_of(b), lambda i, s: step(b + 1, s, count=half, masked=True),
            jnp.zeros((DH, tile), F32),
        )

        @pl.when(b + 1 < n)
        def _():
            send_kv(b + 1)

        dqt = step(b, dqt, masked=True)
        dqt = lax.fori_loop(0, b, step, dqt)
        result = (dqt * scale).T.astype(BF16)

        @pl.when(b == me)
        def _():
            dq_ref[rows(my_s), cols(my_h)] = result

        @pl.when(b != me)
        def _():
            dqs[b] = result
            dq_copy(b, me).start()

        return unused

    lax.fori_loop(0, n, backward_tile, 0)
    send_kv(0)

    for copy in halos + fg_halos:
        copy.wait_recv()

    span = tok + 2 * EDGE
    frame = lax.broadcasted_iota(jnp.int32, (channels, span), 1) + me * tok - EDGE
    inside = (frame >= 0) & (frame < n * tok)
    emg_all = jnp.where(inside, emg_pad[...].astype(F32), 0.0)
    fg_all = jnp.where(inside, fg_pad[...].astype(F32), 0.0)
    filtered = jnp.zeros((channels, tok), F32)
    emg_acc = jnp.zeros((channels, tok), F32)
    for j in range(TAPS):
        tap = taps_pad[j].astype(F32)
        moved = pltpu.roll(emg_all, (REACH - j) % span, 1)
        filtered = filtered + (tap * moved)[:, EDGE:last]
        prod = jnp.where(inside, tap * fg_all, 0.0)
        emg_acc = emg_acc + pltpu.roll(prod, (j - REACH) % span, 1)[:, EDGE:last]
    demg_ref[...] = emg_acc.astype(BF16)
    rows_filtered = filtered.T.astype(BF16)

    @pl.loop(1, m)
    def _(d):
        po_copy(hd, (hd + d) % m).wait_recv()

    total = dot(rows_filtered, ew_ref[:, wide(hd)])
    for d in range(m):
        total = total + pr[d].astype(F32)
    out_ref[...] = total.astype(BF16)

    @pl.loop(1, n)
    def _(d):
        src = (me + d) % n
        dq_copy(me, src).wait_recv()
        for copy in kv_copies(me, src):
            copy.wait_recv()

    for h in range(hc):
        key_sum = jnp.zeros((tok, DH), F32)
        value_sum = jnp.zeros((tok, DH), F32)
        for s in range(g):
            key_sum = key_sum + dkr[h * g + s].astype(F32)
            value_sum = value_sum + dvr[h * g + s].astype(F32)
        dk_ref[:, h * DH:(h + 1) * DH] = (key_sum * scale).astype(BF16)
        dv_ref[:, h * DH:(h + 1) * DH] = value_sum.astype(BF16)

    @pl.loop(1, n)
    def _(d):
        t = (me + d) % n
        for copy in in_copies(t, me) + kv_copies(t, me):
            copy.wait_send()
        ar_copy(t, me).wait_send()
        do_copy(t, me).wait_send()
        dq_copy(t, me).wait_send()

    @pl.loop(1, m)
    def _(d):
        t = (hd + d) % m
        dg_copy(t, hd).wait_send()
        po_copy(t, hd).wait_send()

    for copy in halos + fg_halos:
        copy.wait_send()


def body(n, m, q, k, v, seg, w, emg, taps, ew, do):
    tok, width = q.shape
    hc = width // DH
    g = n // hc
    tile = tok // g
    colw = do.shape[1]
    ch = ew.shape[0]
    span = tok + 2 * EDGE
    segq = seg.reshape(n * g, 1, tile)
    segk = seg.reshape(n, tok, 1)
    vmem = pl.BlockSpec(memory_space=pltpu.VMEM)
    dma = pltpu.SemaphoreType.DMA

    def buf(shape, dtype=BF16):
        return pltpu.VMEM(shape, dtype)

    scratch = [
        buf((n, tile, DH)), buf((n, tok, DH)), buf((n, tok, DH)),
        buf((n, DH, tok)), buf((n, DH, tok)),
        buf((n, tile, DH)), buf((n, 1, tile), F32), buf((tok, width)),
        buf((m, tok, colw)), buf((m, tok, colw)), buf((m, tok, colw)),
        buf((tok, width), F32), buf((tok, width)), buf((n, tile, DH)),
        buf((n, tok, DH), F32), buf((n, tok, DH), F32),
        buf((n, tile, DH)), buf((n, tok, DH)), buf((n, tok, DH)),
        buf((n, tok, DH)), buf((n, tok, DH)),
        buf((ch, span)), buf((TAPS, ch, span)), buf((ch, span)),
        dma((3, n)), dma((3, n)), dma((n,)), dma((n,)), dma((m,)), dma((m,)),
        dma((m,)), dma((m,)), dma((n,)), dma((n,)), dma((n,)), dma((n,)),
        dma((2, n)), dma((2, n)), dma((3, 2)), dma((3, 2)),
    ]
    shapes = [(tok, colw), (tok, width), (tok, width), (tok, width), (ch, tok)]
    return tuple(pl.pallas_call(
        functools.partial(kernel, n, m, hc, g),
        out_shape=[jax.ShapeDtypeStruct(s, BF16) for s in shapes],
        in_specs=[vmem] * 10,
        out_specs=[vmem] * 5,
        scratch_shapes=scratch,
        compiler_params=pltpu.CompilerParams(
            collective_id=0, has_side_effects=True, vmem_limit_bytes=56 * 2**20
        ),
    )(q, k, v, segq, segk, w, emg, taps, ew, do))


def solution(mesh):
    n, m = mesh.shape["ctx"], mesh.shape["head"]
    rows = P("ctx", "head")
    in_specs = (
        rows, rows, rows, P(), P("head", None), P(None, "ctx"), P(None, None, "ctx"), P(), rows,
    )
    out_specs = (rows, rows, rows, rows, P(None, "ctx"))
    return jax.shard_map(
        functools.partial(body, n, m), mesh=mesh, in_specs=in_specs, out_specs=out_specs,
        check_vma=False,
    )
```

time: 493 us -> 138 us (0.28)
  waiting for transfers between devices: 172 us -> 0 us
  matrix products: 157 us -> 0 us
  Pallas kernels: 0 us -> 125 us
  other arithmetic: 60.7 us -> 0 us
  local copies, waits for them, and re-layouts: 57.4 us -> 10.1 us
  starting transfers between devices: 26.1 us -> 0 us
  between operations: 13.9 us -> 0.67 us
    dot_general x46 -> x0, matrix products: 157 us -> none  [the longest x8 34.2 us: gradient_block(): jnp.einsum('qhd,khd->hqk', grad_heads, value_heads, preferred_element_typ...]
    pallas_call x0 -> x1, Pallas kernels: none -> 125 us  [body(): pl.pallas_call(functools.partial(kernel, n, m, hc, g), out_shape=[jax.Sha...]
    ppermute x36 -> x0, waiting for transfers between devices: 113 us -> none  [the longest x32 113 us: shifted(): return lax.ppermute(value, axis, pairs)]
    all_gather x3 -> x0, waiting for transfers between devices: 58.4 us -> none  [the longest x1 27.1 us: body(): grad_cols = lax.all_gather(out_grad, 'head', axis=1, tiled=True)]
    convert_element_type x17 -> x0, other arithmetic: 34.9 us -> none  [the longest x8 16.7 us: key_turn(): shifted((value_grad + value_part).astype(jnp.bfloat16), 'ctx', 1)]
    while x80 -> x0, local copies, waits for them, and re-layouts: 28.9 us -> none
    ppermute x36 -> x0, starting transfers between devices: 26 us -> none  [the longest x32 18.7 us: shifted(): return lax.ppermute(value, axis, pairs)]
    reduce_sum x1 -> x0, other arithmetic: 15.9 us -> none  [body(): new_total = jnp.sum(weights, axis=2)]
  transfers between devices with their start and end apart: 40 -> 0, of which waited for: 35 -> 0; matrix products, arithmetic and copies ran while one was open for 55% -> 0% of each run, Pallas kernels for 0% -> 0%
where the time goes in v1:
time: 138 us; the launch traced here: 136 us
  Pallas kernels  125 us (91%)
  local copies, waits for them, and re-layouts  10.1 us (7%)
    pallas_call x1, Pallas kernels, body(): pl.pallas_call(functools.partial(kernel, n, m, hc, g), out_shape=[jax.Sha...  125 us
    unnamed x11, local copies, waits for them, and re-layouts  6.05 us
    reshape x1, local copies, waits for them, and re-layouts, body(): segk = seg.reshape(n, tok, 1)  4.01 us

profile of v1, /device:TPU:8, one launch (start us, length us, event | category | flops | bytes accessed | tf_op | source)
XLA Modules:
  0.0 135.8 jit_solution(9438061640927455436)
XLA Ops:
  0.6 4.0 %reshape.18.segk_ref = s32[8,512,1]{2,1,0:T(8,128)} reshape(s32[4096]{0:T(1024)} %param.12) | data formatting | bytes 32768 | tf_op jit(solution)/shard_map/reshape | solution.py:381
  4.6 125.1 %shard_map.128 = (bf16[512,512]{1,0:T(8,128)(2,1)}, bf16[512,512]{1,0:T(8,128)(2,1)}, bf16[512,512]{1,0:T(8,128)(2,1)}, bf16[512,512]{1,0:T(8,128)(2,1)}, bf16[64,512]{1,0:T(8,128)(2,1)}) custom-call(bf16[512,512]{1,0:T(8,128)(2,1)} %q_ref.1, bf16[512,512]{1,0:T(8,128)(2,1)} %k_ref.1, bf16[512,512]{1,0:T(8,128)(2,1)} %v_ref.1, s32[16,1,256]{2,1,0:T(1,128)} %bitcast.1, ...), custom_call_target="tpu_custom_call" | custom-call | tf_op jit(solution)/shard_map/pallas_call | solution.py:403
  129.7 0.0 copy-start.1
  129.7 0.0 copy-start
  129.7 0.0 copy-start.2
  129.7 2.0 %copy.20 = bf16[512,512]{1,0:T(8,128)(2,1)} copy(bf16[512,512]{1,0:T(8,128)(2,1)} %get-tuple-element.10) | data formatting | bytes 1048576
  131.7 1.9 %copy.21 = bf16[512,512]{1,0:T(8,128)(2,1)} copy(bf16[512,512]{1,0:T(8,128)(2,1)} %get-tuple-element.11) | data formatting | bytes 1048576
  133.6 0.0 copy-done.1
  133.6 0.8 copy.22
  134.3 0.0 copy-done
  134.3 0.8 copy.23
  135.1 0.0 copy-done.2
  135.1 0.6 copy.24
Async XLA Ops:
  129.7 3.9 %copy-start.1 = (bf16[512,512]{1,0:T(8,128)(2,1)S(1)}, bf16[512,512]{1,0:T(8,128)(2,1)}, u32[]{:S(2)}) copy-start(bf16[512,512]{1,0:T(8,128)(2,1)} %get-tuple-element.12) | copy-start | bytes 1572868
  129.7 4.6 %copy-start = (bf16[512,512]{1,0:T(8,128)(2,1)S(1)}, bf16[512,512]{1,0:T(8,128)(2,1)}, u32[]{:S(2)}) copy-start(bf16[512,512]{1,0:T(8,128)(2,1)} %get-tuple-element.13) | copy-start | bytes 1572868
  129.7 5.4 %copy-start.2 = (bf16[64,512]{1,0:T(8,128)(2,1)S(1)}, bf16[64,512]{1,0:T(8,128)(2,1)}, u32[]{:S(2)}) copy-start(bf16[64,512]{1,0:T(8,128)(2,1)} %get-tuple-element.14) | copy-start | bytes 196612

commit v2 on v1

--- a/solution.py
+++ b/solution.py
@@ -26,12 +26,12 @@
 
 def kernel(
     n, m, hc, g,
-    q_ref, k_ref, v_ref, segq_ref, segk_ref, w_ref, emg_ref, taps_ref, ew_ref, do_ref,
+    q_ref, k_ref, v_ref, segq_ref, seg_ref, w_ref, emg_ref, taps_ref, ew_ref, do_ref,
     out_ref, dq_ref, dk_ref, dv_ref, demg_ref,
     qg, kg, vg, kt, vt, og, lse_s, ar, po, pr, dg, acc_s, ag, dog,
-    dka, dva, dqs, dks, dvs, dkr, dvr, emg_pad, taps_pad, fg_pad,
+    dka, dva, dqs, dks, dvs, dkr, dvr, dkf, dvf, segk_ref, emg_pad, taps_pad, fg_pad,
     s_in, r_in, s_ar, r_ar, s_dg, r_dg, s_po, r_po, s_do, r_do,
-    s_dq, r_dq, s_kv, r_kv, s_halo, r_halo,
+    s_dq, r_dq, s_kv, r_kv, s_sib, r_sib, s_part, r_part, s_halo, r_halo,
 ):
     me = lax.axis_index("ctx")
     hd = lax.axis_index("head")
@@ -71,9 +71,9 @@
     def in_copies(t, src):
         h, s = t // g, t % g
         return (
-            remote(k_ref.at[:, cols(h)], kg.at[src], s_in.at[0, t], r_in.at[0, src], ctx=t),
+            remote(k_ref.at[rows(s), cols(h)], kg.at[src, rows(s)], s_in.at[0, t], r_in.at[0, src], ctx=t),
             remote(q_ref.at[rows(s), cols(h)], qg.at[src], s_in.at[1, t], r_in.at[1, src], ctx=t),
-            remote(v_ref.at[:, cols(h)], vg.at[src], s_in.at[2, t], r_in.at[2, src], ctx=t),
+            remote(v_ref.at[rows(s), cols(h)], vg.at[src, rows(s)], s_in.at[2, t], r_in.at[2, src], ctx=t),
         )
 
     def dg_copy(t, src):
@@ -93,8 +93,22 @@
 
     def kv_copies(t, src):
         return (
-            remote(dks.at[t], dkr.at[src], s_kv.at[0, t], r_kv.at[0, src], ctx=t),
-            remote(dvs.at[t], dvr.at[src], s_kv.at[1, t], r_kv.at[1, src], ctx=t),
+            remote(dkf.at[t], dk_ref.at[rows(src % g), cols(src // g)], s_kv.at[0, t], r_kv.at[0, src], ctx=t),
+            remote(dvf.at[t], dv_ref.at[rows(src % g), cols(src // g)], s_kv.at[1, t], r_kv.at[1, src], ctx=t),
+        )
+
+    def sib_copies(to, frm, b):
+        return tuple(
+            remote(ref.at[b, rows(frm)], ref.at[b, rows(frm)], s_sib.at[i, to, b], r_sib.at[i, frm, b],
+                   ctx=my_h * g + to)
+            for i, ref in enumerate((kg, vg))
+        )
+
+    def part_copies(to, frm, c):
+        return tuple(
+            remote(src.at[c, rows(to)], dst.at[c, frm], s_part.at[i, to, c], r_part.at[i, frm, c],
+                   ctx=my_h * g + to)
+            for i, (src, dst) in enumerate(((dks, dkr), (dvs, dvr)))
         )
 
     right, left = (me + 1) % n, (me + n - 1) % n
@@ -118,8 +132,8 @@
         for copy in in_copies((me + d) % n, me):
             copy.start()
 
-    kg[me] = k_ref[:, cols(my_h)]
-    vg[me] = v_ref[:, cols(my_h)]
+    kg[me, rows(my_s), :] = k_ref[rows(my_s), cols(my_h)]
+    vg[me, rows(my_s), :] = v_ref[rows(my_s), cols(my_h)]
     qg[me] = q_ref[rows(my_s), cols(my_h)]
     dg[hd] = do_ref[...]
     emg_pad[:, EDGE:last] = emg_ref[...]
@@ -130,10 +144,25 @@
     dka[...] = jnp.zeros_like(dka)
     dva[...] = jnp.zeros_like(dva)
 
+    @pl.loop(0, n)
+    def _(c):
+        segk_ref[c] = jnp.broadcast_to(seg_ref[c], (8, tok)).T[:, :1]
+
+    def pass_on(b):
+        @pl.when(b != me)
+        def _():
+            for copy in in_copies(me, b):
+                copy.wait_recv()
+
+        @pl.loop(1, g)
+        def _(d):
+            for copy in sib_copies((my_s + d) % g, my_s, b):
+                copy.start()
+
     def arrive(b):
-        @pl.when(b != me)
-        def _():
-            for copy in in_copies(me, b):
+        @pl.loop(1, g)
+        def _(d):
+            for copy in sib_copies(my_s, (my_s + d) % g, b):
                 copy.wait_recv()
 
         kt[b] = kg[b].T
@@ -153,9 +182,15 @@
     def extra_of(b):
         return jnp.where(b + 1 < n, need_next, 0)
 
+    pass_on(0)
+    pass_on(1)
     arrive(0)
 
     def forward_tile(b, unused):
+        @pl.when(b + 2 < n)
+        def _():
+            pass_on(b + 2)
+
         @pl.when(b + 1 < n)
         def _():
             arrive(b + 1)
@@ -244,18 +279,34 @@
     for copy in fg_halos:
         copy.start()
 
+    def send_parts(c):
+        dks[c] = dka[c].astype(BF16)
+        dvs[c] = dva[c].astype(BF16)
+
+        @pl.loop(1, g)
+        def _(d):
+            for copy in part_copies((my_s + d) % g, my_s, c):
+                copy.start()
+
     def send_kv(c):
-        key_part, value_part = dka[c].astype(BF16), dva[c].astype(BF16)
+        def add(d, sums):
+            frm = (my_s + d) % g
+            for copy in part_copies(my_s, frm, c):
+                copy.wait_recv()
+            return sums[0] + dkr[c, frm].astype(F32), sums[1] + dvr[c, frm].astype(F32)
+
+        sums = lax.fori_loop(1, g, add, (dka[c, rows(my_s), :], dva[c, rows(my_s), :]))
+        key_part, value_part = (sums[0] * scale).astype(BF16), sums[1].astype(BF16)
 
         @pl.when(c == me)
         def _():
-            dkr[me] = key_part
-            dvr[me] = value_part
+            dk_ref[rows(my_s), cols(my_h)] = key_part
+            dv_ref[rows(my_s), cols(my_h)] = value_part
 
         @pl.when(c != me)
         def _():
-            dks[c] = key_part
-            dvs[c] = value_part
+            dkf[c] = key_part
+            dvf[c] = value_part
             for copy in kv_copies(c, me):
                 copy.start()
 
@@ -286,7 +337,7 @@
 
         @pl.when(b + 1 < n)
         def _():
-            send_kv(b + 1)
+            send_parts(b + 1)
 
         dqt = step(b, dqt, masked=True)
         dqt = lax.fori_loop(0, b, step, dqt)
@@ -301,9 +352,14 @@
             dqs[b] = result
             dq_copy(b, me).start()
 
+        @pl.when(b + 1 < n)
+        def _():
+            send_kv(b + 1)
+
         return unused
 
     lax.fori_loop(0, n, backward_tile, 0)
+    send_parts(0)
     send_kv(0)
 
     for copy in halos + fg_halos:
@@ -341,14 +397,14 @@
         for copy in kv_copies(me, src):
             copy.wait_recv()
 
-    for h in range(hc):
-        key_sum = jnp.zeros((tok, DH), F32)
-        value_sum = jnp.zeros((tok, DH), F32)
-        for s in range(g):
-            key_sum = key_sum + dkr[h * g + s].astype(F32)
-            value_sum = value_sum + dvr[h * g + s].astype(F32)
-        dk_ref[:, h * DH:(h + 1) * DH] = (key_sum * scale).astype(BF16)
-        dv_ref[:, h * DH:(h + 1) * DH] = value_sum.astype(BF16)
+    @pl.loop(1, g)
+    def _(d):
+        to = (my_s + d) % g
+
+        @pl.loop(0, n)
+        def _(b):
+            for copy in sib_copies(to, my_s, b) + part_copies(to, my_s, b):
+                copy.wait_send()
 
     @pl.loop(1, n)
     def _(d):
@@ -378,7 +434,7 @@
     ch = ew.shape[0]
     span = tok + 2 * EDGE
     segq = seg.reshape(n * g, 1, tile)
-    segk = seg.reshape(n, tok, 1)
+    segk = seg.reshape(n, 1, tok)
     vmem = pl.BlockSpec(memory_space=pltpu.VMEM)
     dma = pltpu.SemaphoreType.DMA
 
@@ -393,11 +449,12 @@
         buf((tok, width), F32), buf((tok, width)), buf((n, tile, DH)),
         buf((n, tok, DH), F32), buf((n, tok, DH), F32),
         buf((n, tile, DH)), buf((n, tok, DH)), buf((n, tok, DH)),
-        buf((n, tok, DH)), buf((n, tok, DH)),
+        buf((n, g, tile, DH)), buf((n, g, tile, DH)),
+        buf((n, tile, DH)), buf((n, tile, DH)), buf((n, tok, 1), jnp.int32),
         buf((ch, span)), buf((TAPS, ch, span)), buf((ch, span)),
         dma((3, n)), dma((3, n)), dma((n,)), dma((n,)), dma((m,)), dma((m,)),
         dma((m,)), dma((m,)), dma((n,)), dma((n,)), dma((n,)), dma((n,)),
-        dma((2, n)), dma((2, n)), dma((3, 2)), dma((3, 2)),
+        dma((2, n)), dma((2, n)), dma((2, g, n)), dma((2, g, n)), dma((2, g, n)), dma((2, g, n)), dma((3, 2)), dma((3, 2)),
     ]
     shapes = [(tok, colw), (tok, width), (tok, width), (tok, width), (ch, tok)]
     return tuple(pl.pallas_call(

time: 138 us -> 120 us (0.87); the launches traced: 136 us -> 120 us
  Pallas kernels: 125 us -> 113 us
  local copies, waits for them, and re-layouts: 10.1 us -> 6.05 us
    pallas_call x1, Pallas kernels: 125 us -> 113 us  [body(): pl.pallas_call(functools.partial(kernel, n, m, hc, g), out_shape=[jax.Sha...]
    reshape x1 -> x0, local copies, waits for them, and re-layouts: 4.01 us -> none  [body(): segk = seg.reshape(n, tok, 1)]
where the time goes in v2:
time: 120 us
  Pallas kernels  113 us (94%)
  local copies, waits for them, and re-layouts  6.05 us (5%)
    pallas_call x1, Pallas kernels, body(): pl.pallas_call(functools.partial(kernel, n, m, hc, g), out_shape=[jax.Sha...  113 us
    unnamed x11, local copies, waits for them, and re-layouts  6.05 us

profile of v2, /device:TPU:8, one launch (start us, length us, event | category | flops | bytes accessed | tf_op | source)
XLA Modules:
  0.0 120.2 jit_solution(17946840938010592814)
XLA Ops:
  0.6 113.4 %shard_map.128 = (bf16[512,512]{1,0:T(8,128)(2,1)}, bf16[512,512]{1,0:T(8,128)(2,1)}, bf16[512,512]{1,0:T(8,128)(2,1)}, bf16[512,512]{1,0:T(8,128)(2,1)}, bf16[64,512]{1,0:T(8,128)(2,1)}) custom-call(bf16[512,512]{1,0:T(8,128)(2,1)} %q_ref.1, bf16[512,512]{1,0:T(8,128)(2,1)} %k_ref.1, bf16[512,512]{1,0:T(8,128)(2,1)} %v_ref.1, s32[16,1,256]{2,1,0:T(1,128)} %bitcast.2, ...), custom_call_target="tpu_custom_call" | custom-call | tf_op jit(solution)/shard_map/pallas_call | solution.py:460
  114.1 0.0 copy-start.1
  114.1 0.0 copy-start
  114.1 0.0 copy-start.2
  114.1 2.0 %copy.19 = bf16[512,512]{1,0:T(8,128)(2,1)} copy(bf16[512,512]{1,0:T(8,128)(2,1)} %get-tuple-element.10) | data formatting | bytes 1048576
  116.1 1.9 %copy.20 = bf16[512,512]{1,0:T(8,128)(2,1)} copy(bf16[512,512]{1,0:T(8,128)(2,1)} %get-tuple-element.11) | data formatting | bytes 1048576
  117.9 0.0 copy-done.1
  117.9 0.8 copy.21
  118.7 0.0 copy-done
  118.7 0.8 copy.22
  119.5 0.0 copy-done.2
  119.5 0.6 copy.23
Async XLA Ops:
  114.1 3.9 %copy-start.1 = (bf16[512,512]{1,0:T(8,128)(2,1)S(1)}, bf16[512,512]{1,0:T(8,128)(2,1)}, u32[]{:S(2)}) copy-start(bf16[512,512]{1,0:T(8,128)(2,1)} %get-tuple-element.12) | copy-start | bytes 1572868
  114.1 4.6 %copy-start = (bf16[512,512]{1,0:T(8,128)(2,1)S(1)}, bf16[512,512]{1,0:T(8,128)(2,1)}, u32[]{:S(2)}) copy-start(bf16[512,512]{1,0:T(8,128)(2,1)} %get-tuple-element.13) | copy-start | bytes 1572868
  114.1 5.4 %copy-start.2 = (bf16[64,512]{1,0:T(8,128)(2,1)S(1)}, bf16[64,512]{1,0:T(8,128)(2,1)}, u32[]{:S(2)}) copy-start(bf16[64,512]{1,0:T(8,128)(2,1)} %get-tuple-element.14) | copy-start | bytes 196612

commit v3 on v2

--- a/solution.py
+++ b/solution.py
@@ -29,7 +29,7 @@
     q_ref, k_ref, v_ref, segq_ref, seg_ref, w_ref, emg_ref, taps_ref, ew_ref, do_ref,
     out_ref, dq_ref, dk_ref, dv_ref, demg_ref,
     qg, kg, vg, kt, vt, og, lse_s, ar, po, pr, dg, acc_s, ag, dog,
-    dka, dva, dqs, dks, dvs, dkr, dvr, dkf, dvf, segk_ref, emg_pad, taps_pad, fg_pad,
+    dka, dva, dqs, dks, dvs, dkr, dvr, dkf, dvf, dqa, delta_s, segk_ref, emg_pad, taps_pad, fg_pad,
     s_in, r_in, s_ar, r_ar, s_dg, r_dg, s_po, r_po, s_do, r_do,
     s_dq, r_dq, s_kv, r_kv, s_sib, r_sib, s_part, r_part, s_halo, r_halo,
 ):
@@ -234,24 +234,6 @@
 
     lax.fori_loop(0, n, forward_tile, 0)
 
-    @pl.loop(1, n)
-    def _(d):
-        ar_copy(me, (me + d) % n).wait_recv()
-
-    @pl.loop(1, m + 1)
-    def _(d):
-        t = (hd + d) % m
-        part = dot(ar[...], w_ref[:, wide(t)]).astype(BF16)
-
-        @pl.when(t == hd)
-        def _():
-            pr[hd] = part
-
-        @pl.when(t != hd)
-        def _():
-            po[t] = part
-            po_copy(t, hd).start()
-
     acc_s[...] = jnp.zeros_like(acc_s)
     channels = ew_ref.shape[0]
 
@@ -278,6 +260,24 @@
     fg_halos = halo_copies(2, fg_pad, ())
     for copy in fg_halos:
         copy.start()
+
+    @pl.loop(1, n)
+    def _(d):
+        ar_copy(me, (me + d) % n).wait_recv()
+
+    @pl.loop(1, m + 1)
+    def _(d):
+        t = (hd + d) % m
+        part = dot(ar[...], w_ref[:, wide(t)]).astype(BF16)
+
+        @pl.when(t == hd)
+        def _():
+            pr[hd] = part
+
+        @pl.when(t != hd)
+        def _():
+            po[t] = part
+            po_copy(t, hd).start()
 
     def send_parts(c):
         dks[c] = dka[c].astype(BF16)
@@ -310,38 +310,54 @@
             for copy in kv_copies(c, me):
                 copy.start()
 
-    def backward_tile(turn, unused):
-        b = n - 1 - turn
-
+    @pl.loop(0, n)
+    def _(b):
         @pl.when(b != me)
         def _():
             do_copy(me, b).wait_recv()
 
-        q, do, lse = qg[b], dog[b], lse_s[b]
-        delta = jnp.sum((do.astype(F32) * og[b].astype(F32)).T, axis=0, keepdims=True)
-
-        def step(c, dqt, count=tok, masked=False):
-            keys = pl.ds(0, count)
-            st = scores_of(b, c, count, masked, q)
-            p = jnp.exp2(st - lse)
-            dpt = dot(vg[c, keys, :], do, 1, 1)
-            ds = (p * (dpt - delta)).astype(BF16)
-            dva[c, keys, :] += dot(p.astype(BF16), do)
-            dka[c, keys, :] += dot(ds, q)
-            return dqt + dot(kt[c, :, keys], ds)
-
-        dqt = lax.fori_loop(
-            0, extra_of(b), lambda i, s: step(b + 1, s, count=half, masked=True),
-            jnp.zeros((DH, tile), F32),
-        )
-
-        @pl.when(b + 1 < n)
-        def _():
-            send_parts(b + 1)
-
-        dqt = step(b, dqt, masked=True)
-        dqt = lax.fori_loop(0, b, step, dqt)
-        result = (dqt * scale).T.astype(BF16)
+        terms = dog[b].astype(F32) * og[b].astype(F32)
+        delta_s[b] = jnp.sum(terms.T, axis=0, keepdims=True)
+        dqa[b] = jnp.zeros((DH, tile), F32)
+
+    def backward_step(c, b, count=tok, masked=False):
+        keys = pl.ds(0, count)
+        q, do = qg[b], dog[b]
+        st = scores_of(b, c, count, masked, q)
+        p = jnp.exp2(st - lse_s[b])
+        dpt = dot(vg[c, keys, :], do, 1, 1)
+        ds = (p * (dpt - delta_s[b])).astype(BF16)
+        dva[c, keys, :] += dot(p.astype(BF16), do)
+        dka[c, keys, :] += dot(ds, q)
+        dqa[b] += dot(kt[c, :, keys], ds)
+
+    def ordered(turn):
+        return (turn + (my_h + 1) * g) % n
+
+    @pl.loop(0, n)
+    def _(turn):
+        c = ordered(turn)
+
+        @pl.loop(0, jnp.where(c > 0, need_next, 0))
+        def _(i):
+            backward_step(c, c - 1, count=half, masked=True)
+
+        backward_step(c, c, masked=True)
+
+        @pl.loop(c + 1, n)
+        def _(b):
+            backward_step(c, b)
+
+        send_parts(c)
+
+        @pl.when(turn > 0)
+        def _():
+            send_kv(ordered(turn + n - 1))
+
+    @pl.loop(0, n)
+    def _(turn):
+        b = ordered(turn)
+        result = (dqa[b] * scale).T.astype(BF16)
 
         @pl.when(b == me)
         def _():
@@ -352,15 +368,7 @@
             dqs[b] = result
             dq_copy(b, me).start()
 
-        @pl.when(b + 1 < n)
-        def _():
-            send_kv(b + 1)
-
-        return unused
-
-    lax.fori_loop(0, n, backward_tile, 0)
-    send_parts(0)
-    send_kv(0)
+    send_kv(ordered(n - 1))
 
     for copy in halos + fg_halos:
         copy.wait_recv()
@@ -450,7 +458,8 @@
         buf((n, tok, DH), F32), buf((n, tok, DH), F32),
         buf((n, tile, DH)), buf((n, tok, DH)), buf((n, tok, DH)),
         buf((n, g, tile, DH)), buf((n, g, tile, DH)),
-        buf((n, tile, DH)), buf((n, tile, DH)), buf((n, tok, 1), jnp.int32),
+        buf((n, tile, DH)), buf((n, tile, DH)), buf((n, DH, tile), F32),
+        buf((n, 1, tile), F32), buf((n, tok, 1), jnp.int32),
         buf((ch, span)), buf((TAPS, ch, span)), buf((ch, span)),
         dma((3, n)), dma((3, n)), dma((n,)), dma((n,)), dma((m,)), dma((m,)),
         dma((m,)), dma((m,)), dma((n,)), dma((n,)), dma((n,)), dma((n,)),

time: 120 us -> 112 us (0.933); the launches traced: 120 us -> 111 us
  Pallas kernels: 113 us -> 104 us
    pallas_call x1, Pallas kernels: 113 us -> 104 us  [body(): pl.pallas_call(functools.partial(kernel, n, m, hc, g), out_shape=[jax.Sha...]
where the time goes in v3:
time: 112 us; the launch traced here: 111 us
  Pallas kernels  104 us (93%)
  local copies, waits for them, and re-layouts  6.05 us (5%)
    pallas_call x1, Pallas kernels, body(): pl.pallas_call(functools.partial(kernel, n, m, hc, g), out_shape=[jax.Sha...  104 us
    unnamed x11, local copies, waits for them, and re-layouts  6.05 us

profile of v3, /device:TPU:8, one launch (start us, length us, event | category | flops | bytes accessed | tf_op | source)
XLA Modules:
  0.0 110.5 jit_solution(7018543130307367825)
XLA Ops:
  0.6 103.8 %shard_map.128 = (bf16[512,512]{1,0:T(8,128)(2,1)}, bf16[512,512]{1,0:T(8,128)(2,1)}, bf16[512,512]{1,0:T(8,128)(2,1)}, bf16[512,512]{1,0:T(8,128)(2,1)}, bf16[64,512]{1,0:T(8,128)(2,1)}) custom-call(bf16[512,512]{1,0:T(8,128)(2,1)} %q_ref.1, bf16[512,512]{1,0:T(8,128)(2,1)} %k_ref.1, bf16[512,512]{1,0:T(8,128)(2,1)} %v_ref.1, s32[16,1,256]{2,1,0:T(1,128)} %bitcast.2, ...), custom_call_target="tpu_custom_call" | custom-call | tf_op jit(solution)/shard_map/pallas_call | solution.py:469
  104.4 0.0 copy-start.1
  104.5 0.0 copy-start
  104.5 0.0 copy-start.2
  104.5 2.0 %copy.19 = bf16[512,512]{1,0:T(8,128)(2,1)} copy(bf16[512,512]{1,0:T(8,128)(2,1)} %get-tuple-element.10) | data formatting | bytes 1048576
  106.4 1.9 %copy.20 = bf16[512,512]{1,0:T(8,128)(2,1)} copy(bf16[512,512]{1,0:T(8,128)(2,1)} %get-tuple-element.11) | data formatting | bytes 1048576
  108.3 0.0 copy-done.1
  108.3 0.8 copy.21
  109.1 0.0 copy-done
  109.1 0.8 copy.22
  109.9 0.0 copy-done.2
  109.9 0.6 copy.23
Async XLA Ops:
  104.4 3.9 %copy-start.1 = (bf16[512,512]{1,0:T(8,128)(2,1)S(1)}, bf16[512,512]{1,0:T(8,128)(2,1)}, u32[]{:S(2)}) copy-start(bf16[512,512]{1,0:T(8,128)(2,1)} %get-tuple-element.12) | copy-start | bytes 1572868
  104.5 4.6 %copy-start = (bf16[512,512]{1,0:T(8,128)(2,1)S(1)}, bf16[512,512]{1,0:T(8,128)(2,1)}, u32[]{:S(2)}) copy-start(bf16[512,512]{1,0:T(8,128)(2,1)} %get-tuple-element.13) | copy-start | bytes 1572868
  104.5 5.4 %copy-start.2 = (bf16[64,512]{1,0:T(8,128)(2,1)S(1)}, bf16[64,512]{1,0:T(8,128)(2,1)}, u32[]{:S(2)}) copy-start(bf16[64,512]{1,0:T(8,128)(2,1)} %get-tuple-element.14) | copy-start | bytes 196612
